TPU v7x, 256 devices: a whole 4x4x8 slice. The times are simulated.
256 devices in a mesh: ctx: 32 (over y, z), head: 8 (over x, core).
Axes of the slice: x: 4, y: 4, z: 8, core: 2. Of those that a mesh axis runs over, the one named last changes fastest.
Arguments:
- queries: bfloat16 [16384, 1024], P('ctx', 'head'), may hold values from -6 to 6
- keys: bfloat16 [16384, 1024], P('ctx', 'head'), may hold values from -6 to 6
- values: bfloat16 [16384, 1024], P('ctx', 'head'), may hold values from -6 to 6
- gain: float32 [1024], P('head'), may hold values from 0.1 to 1.9
- out_weight: bfloat16 [1024, 1024], P('head'), may hold values from -0.25 to 0.25
Outputs:
- mixed: bfloat16 [16384, 1024], P('ctx', 'head')
All inputs are finite; a program needn't handle non-finite values.
Results may differ from a plain program's by a relative error of at most 0.0065.
Values may be sent and summed in bfloat16 or wider, within the bound.
A program may use at most 128 MiB of HBM per device.

v0:
```python
import functools

import jax
import jax.numpy as jnp
from jax import lax
from jax.experimental import pallas as pl
from jax.experimental.pallas import tpu as pltpu
from jax.sharding import PartitionSpec as P

MESH = pl.DeviceIdType.MESH
DH = 64
LANES = 128
EPSILON = 1e-06
NZ = 8
NY = 4
NH = 8
ROUNDS = 4
EXTRA = 16
F32 = jnp.float32
BF16 = jnp.bfloat16


def nt(a, b):
    return lax.dot_general(a, b, (((1,), (1,)), ((), ())), preferred_element_type=F32)


def nn(a, b):
    return lax.dot_general(a, b, (((1,), (0,)), ((), ())), preferred_element_type=F32)


def rows_of(r):
    return DH + EXTRA if r == 0 else DH


def kernel(q_ref, k_ref, v_ref, gain_ref, w_ref, out_ref,
           kx, kz, qx, qz, vt, qf, num, wbuf, wt, ncat, send1, recv1, ybuf, send2, recv2,
           s1_send, s1_recv, y_send, y_recv, s2_send, s2_recv, w_send, w_recv, n_send, n_recv):
    ctx = lax.axis_index("ctx")
    y, z = ctx // NZ, lax.rem(ctx, NZ)
    me = lax.axis_index("head")
    tok = q_ref.shape[0]

    barrier = pltpu.get_barrier_semaphore()

    def greet(kind, count):
        def body(i, c):
            pl.semaphore_signal(barrier, inc=1, device_id=kind(i), device_id_type=MESH)
            return c
        lax.fori_loop(1, count, body, 0)

    def z_peer(i):
        return {"ctx": y * NZ + lax.rem(z + i, NZ)}

    def y_peer(i):
        return {"ctx": lax.rem(y + i, NY) * NZ + z}

    def h_peer(i):
        return {"head": lax.rem(me + i, NH)}

    greet(z_peer, NZ)
    greet(y_peer, NY)
    greet(h_peer, NH)

    lane = lax.broadcasted_iota(jnp.int32, (tok, LANES), 1)
    low = lane < DH

    def prepare(both, x_ref, z_ref):
        swapped = pltpu.roll(both, DH, 1)
        for h in range(2):
            xx = jnp.where(low, both, swapped) if h == 0 else jnp.where(low, swapped, both)
            x_ref[h] = xx
            z_ref[h] = jnp.where(low, xx, pltpu.roll(xx, DH // 2, 1))

    def product(x_ref, z_ref, h, distance):
        return (z_ref[h] * pltpu.roll(x_ref[h], lax.rem(LANES - distance, LANES), 1)).astype(BF16)

    def middle(both, x_ref):
        shifted = jnp.where(low, pltpu.roll(x_ref[0], LANES - 16, 1), pltpu.roll(x_ref[1], LANES - 16, 1))
        return both * shifted

    keys32 = k_ref[...].astype(F32)
    prepare(keys32, kx, kz)
    vt[...] = jnp.transpose(v_ref[...].astype(F32)).astype(BF16)

    def states(r):
        h, half = r // 2, r % 2
        def body(i, c):
            first = half * 8 + 2 * i
            feats = jnp.concatenate(
                [product(kx, kz, h, first), product(kx, kz, h, first + 1)], axis=1)
            state = nn(vt[h * DH:(h + 1) * DH, :], feats).astype(BF16)
            send1[r, 2 * i, 0:DH, :] = state[:, :LANES]
            send1[r, 2 * i + 1, 0:DH, :] = state[:, LANES:]
            return c
        lax.fori_loop(0, NZ // 2, body, 0)

    def extra_state():
        feats = middle(k_ref[...].astype(F32), kx).astype(BF16)
        pair = nn(vt[...], feats)
        state = jnp.where(low[:DH], pair[:DH], pair[DH:])
        for o in range(NZ):
            piece = jnp.concatenate([state[8 * o:8 * o + 8], jnp.zeros((8, LANES), F32)], axis=0)
            send1[0, o, DH:DH + EXTRA, :] = piece.astype(BF16)

    def columns(i):
        return pl.ds(pl.multiple_of(i * LANES, LANES), LANES)

    def copy(src, dst, sends, recvs, peer):
        return pltpu.make_async_remote_copy(
            src_ref=src, dst_ref=dst, send_sem=sends, recv_sem=recvs, device_id=peer, device_id_type=MESH)

    def z_from(i, arriving):
        return lax.rem(z + NZ - i, NZ) if arriving else z

    def copy1(r, i, arriving=False):
        o, s, n = lax.rem(z + i, NZ), z_from(i, arriving), rows_of(r)
        return copy(send1.at[r, o, pl.ds(0, n)], recv1.at[r, s, pl.ds(0, n)],
                    s1_send.at[r, o], s1_recv.at[r, s], z_peer(i))

    def copy2(r, i, arriving=False):
        o, s, n = lax.rem(z + i, NZ), z_from(i, arriving), rows_of(r)
        return copy(send2.at[r, o, pl.ds(0, n)], recv2.at[r, s, pl.ds(0, n)],
                    s2_send.at[r, o], s2_recv.at[r, s], z_peer(i))

    def copy_y(r, i, arriving=False):
        o, n = lax.rem(y + i, NY), rows_of(r)
        s = lax.rem(y + NY - i, NY) if arriving else y
        return copy(ybuf.at[r, y, pl.ds(0, n)], ybuf.at[r, s, pl.ds(0, n)],
                    y_send.at[r, o], y_recv.at[r, s], y_peer(i))

    def head_from(i, arriving):
        return lax.rem(me + NH - i, NH) if arriving else me

    def copy_w(i, arriving=False):
        o, s = lax.rem(me + i, NH), head_from(i, arriving)
        return copy(w_ref.at[:, columns(o)], wbuf.at[s], w_send.at[o], w_recv.at[s], h_peer(i))

    def copy_n(h, i, arriving=False):
        o, s = lax.rem(me + i, NH), head_from(i, arriving)
        return copy(ncat.at[h, me], ncat.at[h, s], n_send.at[h, o], n_recv.at[h, s], h_peer(i))

    def each(count, do):
        def body(i, c):
            do(i)
            return c
        lax.fori_loop(1, count, body, 0)

    extra_state()
    for r in range(ROUNDS):
        states(r)
        if r == 0:
            pl.semaphore_wait(barrier, NZ + NY + NH - 3)
        each(NZ, lambda i: copy1(r, i).start())
        recv1[r, z, 0:rows_of(r), :] = send1[r, z, 0:rows_of(r), :]
    each(NH, lambda i: copy_w(i).start())
    wbuf[me] = w_ref[:, columns(me)]

    queries32 = q_ref[...].astype(F32) * 0.125
    prepare(queries32, qx, qz)
    for h in range(2):
        qf[h, 0] = product(qx, qz, h, 0)
        qz[h] = qz[h] * 2.0
        mine = low if h == 0 else jnp.logical_not(low)
        qf[h, 16] = jnp.where(mine, middle(queries32 * 2.0, qx), 0.0).astype(BF16)

        def fill(i, c, h=h):
            qf[h, i] = product(qx, qz, h, i)
            return c
        lax.fori_loop(1, 16, fill, 0)

    def intra(h):
        mine = low if h == 0 else jnp.logical_not(low)
        masked = jnp.where(mine, queries32, 0.0).astype(BF16)
        for b in range(2):
            seen, first = 256 * (b + 1), 256 * b
            scores = nt(k_ref[0:seen, :], masked[first:first + 256])
            s_at = lax.broadcasted_iota(jnp.int32, (seen, 256), 0)
            t_at = lax.broadcasted_iota(jnp.int32, (seen, 256), 1) + first
            weights = jnp.where(s_at <= t_at, scores * scores, 0.0).astype(BF16)
            num[h, :, first:first + 256] = nn(vt[h * DH:(h + 1) * DH, 0:seen], weights)

    intra(0)
    intra(1)

    def totals(r):
        n = rows_of(r)
        each(NZ, lambda i: copy1(r, i, True).wait_recv())
        total = recv1[r, 0, 0:n, :].astype(F32)
        for s in range(1, NZ):
            total += recv1[r, s, 0:n, :].astype(F32)
        ybuf[r, y, 0:n, :] = total
        each(NY, lambda i: copy_y(r, i).start())

    def prefixes(r):
        n = rows_of(r)
        each(NY, lambda i: copy_y(r, i, True).wait_recv())
        running = jnp.zeros((n, LANES), F32)
        for s in range(NY):
            running += jnp.where(s < y, ybuf[r, s, 0:n, :], 0.0)
        for s in range(NZ):
            send2[r, s, 0:n, :] = running.astype(BF16)
            running += recv1[r, s, 0:n, :].astype(F32)
        each(NZ, lambda i: copy2(r, i).start())
        recv2[r, z, 0:n, :] = send2[r, z, 0:n, :]

    def read_out(r):
        h, half = r // 2, r % 2
        each(NZ, lambda i: copy2(r, i, True).wait_recv())
        prefix = [recv2[r, o, 0:DH, :] for o in range(NZ)]
        feats = [qf[h, half * 8 + o] for o in range(NZ)]
        if half == 0:
            pieces = [recv2[0, o, DH:DH + EXTRA, :].astype(F32)[:8] for o in range(NZ)]
            prefix.append(jnp.concatenate(pieces, axis=0).astype(BF16))
            feats.append(qf[h, 16])
        num[h] += nt(jnp.concatenate(prefix, axis=1), jnp.concatenate(feats, axis=1))

    gains = jnp.transpose(jnp.broadcast_to(gain_ref[...], (LANES, LANES)))

    def normalise(h):
        value = num[h]
        meansq = jnp.mean(value * value, axis=0, keepdims=True)
        gain = jnp.concatenate([gains[h * DH:(h + 1) * DH]] * (tok // LANES), axis=1)
        ncat[h, me] = (value * lax.rsqrt(meansq + EPSILON) * gain).astype(BF16)
        each(NH, lambda i: copy_n(h, i).start())

    totals(0)
    totals(1)
    prefixes(0)
    totals(2)
    prefixes(1)
    totals(3)
    prefixes(2)
    each(NH, lambda i: copy_w(i, True).wait_recv())
    for s in range(NH):
        wt[:, s * LANES:(s + 1) * LANES] = jnp.transpose(wbuf[s].astype(F32)).astype(BF16)
    prefixes(3)
    read_out(0)
    read_out(1)
    normalise(0)
    read_out(2)
    read_out(3)
    normalise(1)
    for h in range(2):
        each(NH, lambda i: copy_n(h, i, True).wait_recv())
    blocks = jnp.concatenate([ncat[h, s] for s in range(NH) for h in range(2)], axis=0)
    mixed = nn(wt[...], blocks)
    out_ref[...] = jnp.transpose(mixed).astype(BF16)

    for r in range(ROUNDS):
        each(NZ, lambda i: copy1(r, i).wait_send())
        each(NY, lambda i: copy_y(r, i).wait_send())
        each(NZ, lambda i: copy2(r, i).wait_send())
    each(NH, lambda i: copy_w(i).wait_send())
    for h in range(2):
        each(NH, lambda i: copy_n(h, i).wait_send())


def per_device(queries, keys, values, gain, out_weight):
    tok, width = queries.shape
    rows = DH + EXTRA
    vmem = pl.BlockSpec(memory_space=pltpu.VMEM)
    dma = pltpu.SemaphoreType.DMA
    return pl.pallas_call(
        kernel,
        out_shape=jax.ShapeDtypeStruct((tok, width), BF16),
        in_specs=[vmem] * 5,
        out_specs=vmem,
        scratch_shapes=[
            pltpu.VMEM((2, tok, LANES), F32),
            pltpu.VMEM((2, tok, LANES), F32),
            pltpu.VMEM((2, tok, LANES), F32),
            pltpu.VMEM((2, tok, LANES), F32),
            pltpu.VMEM((LANES, tok), BF16),
            pltpu.VMEM((2, 17, tok, LANES), BF16),
            pltpu.VMEM((2, DH, tok), F32),
            pltpu.VMEM((NH, LANES, LANES), BF16),
            pltpu.VMEM((LANES, NH * LANES), BF16),
            pltpu.VMEM((2, NH, DH, tok), BF16),
            pltpu.VMEM((ROUNDS, NZ, rows, LANES), BF16),
            pltpu.VMEM((ROUNDS, NZ, rows, LANES), BF16),
            pltpu.VMEM((ROUNDS, NY, rows, LANES), F32),
            pltpu.VMEM((ROUNDS, NZ, rows, LANES), BF16),
            pltpu.VMEM((ROUNDS, NZ, rows, LANES), BF16),
            dma((ROUNDS, NZ)), dma((ROUNDS, NZ)),
            dma((ROUNDS, NY)), dma((ROUNDS, NY)),
            dma((ROUNDS, NZ)), dma((ROUNDS, NZ)),
            dma((NH,)), dma((NH,)),
            dma((2, NH)), dma((2, NH)),
        ],
        compiler_params=pltpu.CompilerParams(
            collective_id=0, has_side_effects=True, vmem_limit_bytes=40 << 20),
    )(queries, keys, values, gain.reshape(1, width), out_weight)


def solution(mesh):
    return jax.shard_map(
        per_device,
        mesh=mesh,
        in_specs=(P("ctx", "head"), P("ctx", "head"), P("ctx", "head"), P("head"), P("head", None)),
        out_specs=P("ctx", "head"),
        check_vma=False,
    )
```

profile of v0, /device:TPU:1, one launch (start us, length us, event | category | flops | bytes accessed | tf_op | source)
XLA Modules:
  0.0 55.5 jit_solution(11569820975505255909)
XLA Ops:
  0.0 0.0 copy-start.4
  0.0 0.7 %copy-done.4 = f32[128]{0:T(128)S(1)} copy-done((f32[128]{0:T(128)S(1)}, f32[128]{0:T(128)}, u32[]{:S(2)}) %copy-start.4) | copy-done | bytes 536
  0.7 0.0 copy-start
  0.7 0.9 %copy-done = bf16[128,1024]{1,0:T(8,128)(2,1)S(1)} copy-done((bf16[128,1024]{1,0:T(8,128)(2,1)S(1)}, bf16[128,1024]{1,0:T(8,128)(2,1)}, u32[]{:S(2)}) %copy-start) | copy-done | bytes 262168
  1.6 0.0 copy-start.1
  1.6 0.9 %copy-done.1 = bf16[512,128]{1,0:T(8,128)(2,1)S(1)} copy-done((bf16[512,128]{1,0:T(8,128)(2,1)S(1)}, bf16[512,128]{1,0:T(8,128)(2,1)}, u32[]{:S(2)}) %copy-start.1) | copy-done | bytes 131096
  2.5 0.0 copy-start.2
  2.5 0.9 %copy-done.2 = bf16[512,128]{1,0:T(8,128)(2,1)S(1)} copy-done((bf16[512,128]{1,0:T(8,128)(2,1)S(1)}, bf16[512,128]{1,0:T(8,128)(2,1)}, u32[]{:S(2)}) %copy-start.2) | copy-done | bytes 131096
  3.4 0.0 copy-start.3
  3.4 0.9 %copy-done.3 = bf16[512,128]{1,0:T(8,128)(2,1)S(1)} copy-done((bf16[512,128]{1,0:T(8,128)(2,1)S(1)}, bf16[512,128]{1,0:T(8,128)(2,1)}, u32[]{:S(2)}) %copy-start.3) | copy-done | bytes 131096
  4.3 50.5 %shard_map.55 = bf16[512,128]{1,0:T(8,128)(2,1)S(1)} custom-call(bf16[512,128]{1,0:T(8,128)(2,1)S(1)} %copy-done.1, bf16[512,128]{1,0:T(8,128)(2,1)S(1)} %copy-done.2, bf16[512,128]{1,0:T(8,128)(2,1)S(1)} %copy-done.3, f32[1,128]{1,0:T(1,128)S(1)} %bitcast.1, bf16[128,1024]{1,0:T(8,128)(2,1)S(1)} %copy-done), custom_call_target="tpu_custom_call" | custom-call | tf_op jit(solution)/shard_map/pallas_call | solution.py:263
  54.9 0.7 %copy.7 = bf16[512,128]{1,0:T(8,128)(2,1)} copy(bf16[512,128]{1,0:T(8,128)(2,1)S(1)} %shard_map.55) | data formatting | bytes 262144
Async XLA Ops:
  0.0 0.7 %copy-start.4 = (f32[128]{0:T(128)S(1)}, f32[128]{0:T(128)}, u32[]{:S(2)}) copy-start(f32[128]{0:T(128)} %param.8) | copy-start | bytes 1540
  0.7 0.9 %copy-start = (bf16[128,1024]{1,0:T(8,128)(2,1)S(1)}, bf16[128,1024]{1,0:T(8,128)(2,1)}, u32[]{:S(2)}) copy-start(bf16[128,1024]{1,0:T(8,128)(2,1)} %w_ref.1) | copy-start | bytes 786436
  1.6 0.9 %copy-start.1 = (bf16[512,128]{1,0:T(8,128)(2,1)S(1)}, bf16[512,128]{1,0:T(8,128)(2,1)}, u32[]{:S(2)}) copy-start(bf16[512,128]{1,0:T(8,128)(2,1)} %q_ref.1) | copy-start | bytes 393220
  2.5 0.9 %copy-start.2 = (bf16[512,128]{1,0:T(8,128)(2,1)S(1)}, bf16[512,128]{1,0:T(8,128)(2,1)}, u32[]{:S(2)}) copy-start(bf16[512,128]{1,0:T(8,128)(2,1)} %k_ref.1) | copy-start | bytes 393220
  3.4 0.9 %copy-start.3 = (bf16[512,128]{1,0:T(8,128)(2,1)S(1)}, bf16[512,128]{1,0:T(8,128)(2,1)}, u32[]{:S(2)}) copy-start(bf16[512,128]{1,0:T(8,128)(2,1)} %v_ref.1) | copy-start | bytes 393220
where the time goes:
time: 55.7 us; the launch traced here: 55.5 us
  Pallas kernels  50.5 us (91%)
  local copies, waits for them, and re-layouts  4.97 us (9%)
    pallas_call x1, Pallas kernels, per_device(): pl.pallas_call(kernel, out_shape=jax.ShapeDtypeStruct((tok, width), BF16)...  50.5 us
    unnamed x11, local copies, waits for them, and re-layouts  4.97 us

commit v1 on v0

--- a/solution.py
+++ b/solution.py
@@ -32,13 +32,20 @@
     return DH + EXTRA if r == 0 else DH
 
 
-def kernel(q_ref, k_ref, v_ref, gain_ref, w_ref, out_ref,
-           kx, kz, qx, qz, vt, qf, num, wbuf, wt, ncat, send1, recv1, ybuf, send2, recv2,
-           s1_send, s1_recv, y_send, y_recv, s2_send, s2_recv, w_send, w_recv, n_send, n_recv):
+def kernel(q_hbm, k_hbm, v_hbm, gain_hbm, w_hbm, out_ref,
+           q_ref, k_ref, v_ref, gain_ref, w_ref, kx, kz, qx, qz, vt, qf, num, wbuf, wt, acc, ncat, send1, recv1, ybuf, send2, recv2,
+           s1_send, s1_recv, y_send, y_recv, s2_send, s2_recv, w_send, w_recv, n_send, n_recv, p_send, loaded):
     ctx = lax.axis_index("ctx")
     y, z = ctx // NZ, lax.rem(ctx, NZ)
     me = lax.axis_index("head")
     tok = q_ref.shape[0]
+
+    def load(i):
+        pairs = ((k_hbm, k_ref), (v_hbm, v_ref), (q_hbm, q_ref), (w_hbm, w_ref), (gain_hbm, gain_ref))
+        return pltpu.make_async_copy(*pairs[i], loaded.at[i])
+
+    for i in range(5):
+        load(i).start()
 
     barrier = pltpu.get_barrier_semaphore()
 
@@ -71,28 +78,27 @@
             x_ref[h] = xx
             z_ref[h] = jnp.where(low, xx, pltpu.roll(xx, DH // 2, 1))
 
-    def product(x_ref, z_ref, h, distance):
-        return (z_ref[h] * pltpu.roll(x_ref[h], lax.rem(LANES - distance, LANES), 1)).astype(BF16)
+    def products(x_ref, z_ref, h, first, count):
+        fixed = z_ref[h].astype(BF16)
+        turned = [pltpu.roll(x_ref[h], (LANES - d) % LANES, 1) for d in range(first, first + count)]
+        return [fixed * t.astype(BF16) for t in turned]
 
     def middle(both, x_ref):
         shifted = jnp.where(low, pltpu.roll(x_ref[0], LANES - 16, 1), pltpu.roll(x_ref[1], LANES - 16, 1))
         return both * shifted
 
+    load(0).wait()
     keys32 = k_ref[...].astype(F32)
     prepare(keys32, kx, kz)
+    load(1).wait()
     vt[...] = jnp.transpose(v_ref[...].astype(F32)).astype(BF16)
 
     def states(r):
         h, half = r // 2, r % 2
-        def body(i, c):
-            first = half * 8 + 2 * i
-            feats = jnp.concatenate(
-                [product(kx, kz, h, first), product(kx, kz, h, first + 1)], axis=1)
-            state = nn(vt[h * DH:(h + 1) * DH, :], feats).astype(BF16)
-            send1[r, 2 * i, 0:DH, :] = state[:, :LANES]
-            send1[r, 2 * i + 1, 0:DH, :] = state[:, LANES:]
-            return c
-        lax.fori_loop(0, NZ // 2, body, 0)
+        feats = jnp.concatenate(products(kx, kz, h, half * NZ, NZ), axis=1)
+        state = nn(vt[h * DH:(h + 1) * DH, :], feats).astype(BF16)
+        for o in range(NZ):
+            send1[r, o, 0:DH, :] = state[:, o * LANES:(o + 1) * LANES]
 
     def extra_state():
         feats = middle(k_ref[...].astype(F32), kx).astype(BF16)
@@ -136,8 +142,15 @@
         return copy(w_ref.at[:, columns(o)], wbuf.at[s], w_send.at[o], w_recv.at[s], h_peer(i))
 
     def copy_n(h, i, arriving=False):
-        o, s = lax.rem(me + i, NH), head_from(i, arriving)
-        return copy(ncat.at[h, me], ncat.at[h, s], n_send.at[h, o], n_recv.at[h, s], h_peer(i))
+        s = head_from(2 * i, arriving)
+        return copy(ncat.at[h, me], ncat.at[h, s], n_send.at[h, i], n_recv.at[h, s], h_peer(2 * i))
+
+    sibling = {"head": me + 1 - 2 * lax.rem(me, 2)}
+
+    def copy_pair(h, i, arriving=False):
+        held = lax.rem(me + NH - 2 * i, NH)
+        s = held + 1 - 2 * lax.rem(me, 2) if arriving else held
+        return copy(ncat.at[h, held], ncat.at[h, s], p_send.at[h, i], n_recv.at[h, s], sibling)
 
     def each(count, do):
         def body(i, c):
@@ -152,21 +165,20 @@
             pl.semaphore_wait(barrier, NZ + NY + NH - 3)
         each(NZ, lambda i: copy1(r, i).start())
         recv1[r, z, 0:rows_of(r), :] = send1[r, z, 0:rows_of(r), :]
+    load(3).wait()
     each(NH, lambda i: copy_w(i).start())
     wbuf[me] = w_ref[:, columns(me)]
 
+    load(2).wait()
     queries32 = q_ref[...].astype(F32) * 0.125
     prepare(queries32, qx, qz)
     for h in range(2):
-        qf[h, 0] = product(qx, qz, h, 0)
-        qz[h] = qz[h] * 2.0
         mine = low if h == 0 else jnp.logical_not(low)
         qf[h, 16] = jnp.where(mine, middle(queries32 * 2.0, qx), 0.0).astype(BF16)
-
-        def fill(i, c, h=h):
-            qf[h, i] = product(qx, qz, h, i)
-            return c
-        lax.fori_loop(1, 16, fill, 0)
+        qf[h, 0] = products(qx, qz, h, 0, 1)[0]
+        qz[h] = qz[h] * 2.0
+        for i, feats in enumerate(products(qx, qz, h, 1, 15)):
+            qf[h, i + 1] = feats
 
     def intra(h):
         mine = low if h == 0 else jnp.logical_not(low)
@@ -189,23 +201,41 @@
         for s in range(1, NZ):
             total += recv1[r, s, 0:n, :].astype(F32)
         ybuf[r, y, 0:n, :] = total
-        each(NY, lambda i: copy_y(r, i).start())
+        def to_later(i):
+            @pl.when(y + i < NY)
+            def _():
+                copy_y(r, i).start()
+        each(NY, to_later)
 
     def prefixes(r):
         n = rows_of(r)
-        each(NY, lambda i: copy_y(r, i, True).wait_recv())
+        def from_earlier(i):
+            @pl.when(y >= i)
+            def _():
+                copy_y(r, i, True).wait_recv()
+        each(NY, from_earlier)
         running = jnp.zeros((n, LANES), F32)
         for s in range(NY):
             running += jnp.where(s < y, ybuf[r, s, 0:n, :], 0.0)
         for s in range(NZ):
             send2[r, s, 0:n, :] = running.astype(BF16)
             running += recv1[r, s, 0:n, :].astype(F32)
-        each(NZ, lambda i: copy2(r, i).start())
+        def give(i):
+            @pl.when(y + lax.rem(z + i, NZ) > 0)
+            def _():
+                copy2(r, i).start()
+        each(NZ, give)
         recv2[r, z, 0:n, :] = send2[r, z, 0:n, :]
 
     def read_out(r):
         h, half = r // 2, r % 2
-        each(NZ, lambda i: copy2(r, i, True).wait_recv())
+        @pl.when(y + z > 0)
+        def _():
+            each(NZ, lambda i: copy2(r, i, True).wait_recv())
+
+        @pl.when(y + z == 0)
+        def _():
+            recv2[r] = jnp.zeros(recv2.shape[1:], BF16)
         prefix = [recv2[r, o, 0:DH, :] for o in range(NZ)]
         feats = [qf[h, half * 8 + o] for o in range(NZ)]
         if half == 0:
@@ -214,6 +244,7 @@
             feats.append(qf[h, 16])
         num[h] += nt(jnp.concatenate(prefix, axis=1), jnp.concatenate(feats, axis=1))
 
+    load(4).wait()
     gains = jnp.transpose(jnp.broadcast_to(gain_ref[...], (LANES, LANES)))
 
     def normalise(h):
@@ -221,7 +252,19 @@
         meansq = jnp.mean(value * value, axis=0, keepdims=True)
         gain = jnp.concatenate([gains[h * DH:(h + 1) * DH]] * (tok // LANES), axis=1)
         ncat[h, me] = (value * lax.rsqrt(meansq + EPSILON) * gain).astype(BF16)
-        each(NH, lambda i: copy_n(h, i).start())
+        each(NH // 2, lambda i: copy_n(h, i).start())
+        copy_pair(h, 0).start()
+
+    def pass_on(h):
+        for i in (1, 3, 2):
+            copy_n(h, i, True).wait_recv()
+            copy_pair(h, i).start()
+
+    def project(h):
+        for i in range(NH // 2):
+            copy_pair(h, i, True).wait_recv()
+        blocks = jnp.concatenate([ncat[h, s] for s in range(NH)], axis=0)
+        return nn(wt[:, h * NH * DH:(h + 1) * NH * DH], blocks)
 
     totals(0)
     totals(1)
@@ -231,28 +274,39 @@
     totals(3)
     prefixes(2)
     each(NH, lambda i: copy_w(i, True).wait_recv())
-    for s in range(NH):
-        wt[:, s * LANES:(s + 1) * LANES] = jnp.transpose(wbuf[s].astype(F32)).astype(BF16)
+    turned = [jnp.transpose(wbuf[s].astype(F32)) for s in range(NH)]
+    for h in range(2):
+        part = jnp.concatenate([t[:, h * DH:(h + 1) * DH] for t in turned], axis=1)
+        wt[:, h * NH * DH:(h + 1) * NH * DH] = part.astype(BF16)
     prefixes(3)
     read_out(0)
     read_out(1)
     normalise(0)
     read_out(2)
+    pass_on(0)
     read_out(3)
     normalise(1)
-    for h in range(2):
-        each(NH, lambda i: copy_n(h, i, True).wait_recv())
-    blocks = jnp.concatenate([ncat[h, s] for s in range(NH) for h in range(2)], axis=0)
-    mixed = nn(wt[...], blocks)
-    out_ref[...] = jnp.transpose(mixed).astype(BF16)
+    acc[...] = project(0)
+    pass_on(1)
+    out_ref[...] = jnp.transpose(acc[...] + project(1)).astype(BF16)
 
     for r in range(ROUNDS):
         each(NZ, lambda i: copy1(r, i).wait_send())
-        each(NY, lambda i: copy_y(r, i).wait_send())
-        each(NZ, lambda i: copy2(r, i).wait_send())
+        def sent(i, r=r):
+            @pl.when(y + i < NY)
+            def _():
+                copy_y(r, i).wait_send()
+        each(NY, sent)
+        def given(i, r=r):
+            @pl.when(y + lax.rem(z + i, NZ) > 0)
+            def _():
+                copy2(r, i).wait_send()
+        each(NZ, given)
     each(NH, lambda i: copy_w(i).wait_send())
     for h in range(2):
-        each(NH, lambda i: copy_n(h, i).wait_send())
+        each(NH // 2, lambda i: copy_n(h, i).wait_send())
+        for i in range(NH // 2):
+            copy_pair(h, i).wait_send()
 
 
 def per_device(queries, keys, values, gain, out_weight):
@@ -263,9 +317,14 @@
     return pl.pallas_call(
         kernel,
         out_shape=jax.ShapeDtypeStruct((tok, width), BF16),
-        in_specs=[vmem] * 5,
+        in_specs=[pl.BlockSpec(memory_space=pltpu.HBM)] * 5,
         out_specs=vmem,
         scratch_shapes=[
+            pltpu.VMEM((tok, width), BF16),
+            pltpu.VMEM((tok, width), BF16),
+            pltpu.VMEM((tok, width), BF16),
+            pltpu.VMEM((1, width), F32),
+            pltpu.VMEM(out_weight.shape, BF16),
             pltpu.VMEM((2, tok, LANES), F32),
             pltpu.VMEM((2, tok, LANES), F32),
             pltpu.VMEM((2, tok, LANES), F32),
@@ -275,6 +334,7 @@
             pltpu.VMEM((2, DH, tok), F32),
             pltpu.VMEM((NH, LANES, LANES), BF16),
             pltpu.VMEM((LANES, NH * LANES), BF16),
+            pltpu.VMEM((LANES, tok), F32),
             pltpu.VMEM((2, NH, DH, tok), BF16),
             pltpu.VMEM((ROUNDS, NZ, rows, LANES), BF16),
             pltpu.VMEM((ROUNDS, NZ, rows, LANES), BF16),
@@ -285,10 +345,11 @@
             dma((ROUNDS, NY)), dma((ROUNDS, NY)),
             dma((ROUNDS, NZ)), dma((ROUNDS, NZ)),
             dma((NH,)), dma((NH,)),
-            dma((2, NH)), dma((2, NH)),
+            dma((2, NH // 2)), dma((2, NH)), dma((2, NH // 2)),
+            dma((5,)),
         ],
         compiler_params=pltpu.CompilerParams(
-            collective_id=0, has_side_effects=True, vmem_limit_bytes=40 << 20),
+            collective_id=0, has_side_effects=True, vmem_limit_bytes=55040 << 10),
     )(queries, keys, values, gain.reshape(1, width), out_weight)
 
 

time: 55.7 us -> 47.8 us (0.86)
  the two profiles are of different devices: /device:TPU:1 before, /device:TPU:17 now
where the time goes in v1:
time: 47.8 us; the launch traced here: 47.7 us
  Pallas kernels  46.4 us (97%)
  local copies, waits for them, and re-layouts  1.31 us (3%)
    pallas_call x1, Pallas kernels, per_device(): pl.pallas_call(kernel, out_shape=jax.ShapeDtypeStruct((tok, width), BF16)...  46.4 us
    unnamed x3, local copies, waits for them, and re-layouts  1.31 us

profile of v1, /device:TPU:17, one launch (start us, length us, event | category | flops | bytes accessed | tf_op | source)
XLA Modules:
  0.0 47.7 jit_solution(8542505576332603022)
XLA Ops:
  0.0 0.0 copy-start
  0.0 0.7 %copy-done = f32[128]{0:T(128)S(1)} copy-done((f32[128]{0:T(128)S(1)}, f32[128]{0:T(128)}, u32[]{:S(2)}) %copy-start) | copy-done | bytes 536
  0.7 46.4 %shard_map.55 = bf16[512,128]{1,0:T(8,128)(2,1)S(1)} custom-call(bf16[512,128]{1,0:T(8,128)(2,1)} %q_hbm.1, bf16[512,128]{1,0:T(8,128)(2,1)} %k_hbm.1, bf16[512,128]{1,0:T(8,128)(2,1)} %v_hbm.1, f32[1,128]{1,0:T(1,128)S(1)} %bitcast.1, bf16[128,1024]{1,0:T(8,128)(2,1)} %w_hbm.1), custom_call_target="tpu_custom_call" | custom-call | tf_op jit(solution)/shard_map/pallas_call | solution.py:317
  47.0 0.7 %copy.7 = bf16[512,128]{1,0:T(8,128)(2,1)} copy(bf16[512,128]{1,0:T(8,128)(2,1)S(1)} %shard_map.55) | data formatting | bytes 262144
Async XLA Ops:
  0.0 0.7 %copy-start = (f32[128]{0:T(128)S(1)}, f32[128]{0:T(128)}, u32[]{:S(2)}) copy-start(f32[128]{0:T(128)} %param.8) | copy-start | bytes 1540

commit v2 on v1

--- a/solution.py
+++ b/solution.py
@@ -28,13 +28,17 @@
     return lax.dot_general(a, b, (((1,), (0,)), ((), ())), preferred_element_type=F32)
 
 
+FIRST = 48
+ROWS = (DH + EXTRA, DH, 2 * FIRST, 2 * (DH - FIRST))
+
+
 def rows_of(r):
-    return DH + EXTRA if r == 0 else DH
+    return ROWS[r]
 
 
 def kernel(q_hbm, k_hbm, v_hbm, gain_hbm, w_hbm, out_ref,
-           q_ref, k_ref, v_ref, gain_ref, w_ref, kx, kz, qx, qz, vt, qf, num, wbuf, wt, acc, ncat, send1, recv1, ybuf, send2, recv2,
-           s1_send, s1_recv, y_send, y_recv, s2_send, s2_recv, w_send, w_recv, n_send, n_recv, p_send, loaded):
+           q_ref, k_ref, v_ref, gain_ref, w_ref, kx, kz, qx, qz, vt, qf, num, wbuf, wt, wt2, acc, middles, ncat, early, last, send1, recv1, ybuf, send2, recv2,
+           s1_send, s1_recv, y_send, y_recv, s2_send, s2_recv, w_send, w_recv, n_send, n_recv, p_send, l_send, l_recv, loaded):
     ctx = lax.axis_index("ctx")
     y, z = ctx // NZ, lax.rem(ctx, NZ)
     me = lax.axis_index("head")
@@ -93,12 +97,17 @@
     load(1).wait()
     vt[...] = jnp.transpose(v_ref[...].astype(F32)).astype(BF16)
 
-    def states(r):
-        h, half = r // 2, r % 2
+    def states(h, half):
         feats = jnp.concatenate(products(kx, kz, h, half * NZ, NZ), axis=1)
         state = nn(vt[h * DH:(h + 1) * DH, :], feats).astype(BF16)
         for o in range(NZ):
-            send1[r, o, 0:DH, :] = state[:, o * LANES:(o + 1) * LANES]
+            piece = state[:, o * LANES:(o + 1) * LANES]
+            if h == 0:
+                send1[half, o, 0:DH, :] = piece
+            else:
+                last = DH - FIRST
+                send1[2, o, half * FIRST:(half + 1) * FIRST, :] = piece[:FIRST]
+                send1[3, o, half * last:(half + 1) * last, :] = piece[FIRST:]
 
     def extra_state():
         feats = middle(k_ref[...].astype(F32), kx).astype(BF16)
@@ -142,15 +151,19 @@
         return copy(w_ref.at[:, columns(o)], wbuf.at[s], w_send.at[o], w_recv.at[s], h_peer(i))
 
     def copy_n(h, i, arriving=False):
-        s = head_from(2 * i, arriving)
-        return copy(ncat.at[h, me], ncat.at[h, s], n_send.at[h, i], n_recv.at[h, s], h_peer(2 * i))
+        s, held = head_from(2 * i, arriving), (ncat, early)[h]
+        return copy(held.at[me], held.at[s], n_send.at[h, i], n_recv.at[h, s], h_peer(2 * i))
 
     sibling = {"head": me + 1 - 2 * lax.rem(me, 2)}
 
     def copy_pair(h, i, arriving=False):
-        held = lax.rem(me + NH - 2 * i, NH)
-        s = held + 1 - 2 * lax.rem(me, 2) if arriving else held
-        return copy(ncat.at[h, held], ncat.at[h, s], p_send.at[h, i], n_recv.at[h, s], sibling)
+        mine, held = lax.rem(me + NH - 2 * i, NH), (ncat, early)[h]
+        s = mine + 1 - 2 * lax.rem(me, 2) if arriving else mine
+        return copy(held.at[mine], held.at[s], p_send.at[h, i], n_recv.at[h, s], sibling)
+
+    def copy_last(i, arriving=False):
+        s = head_from(i, arriving)
+        return copy(last.at[me], last.at[s], l_send.at[i], l_recv.at[s], h_peer(i))
 
     def each(count, do):
         def body(i, c):
@@ -160,7 +173,11 @@
 
     extra_state()
     for r in range(ROUNDS):
-        states(r)
+        if r < 2:
+            states(0, r)
+        elif r == 2:
+            states(1, 0)
+            states(1, 1)
         if r == 0:
             pl.semaphore_wait(barrier, NZ + NY + NH - 3)
         each(NZ, lambda i: copy1(r, i).start())
@@ -227,8 +244,7 @@
         each(NZ, give)
         recv2[r, z, 0:n, :] = send2[r, z, 0:n, :]
 
-    def read_out(r):
-        h, half = r // 2, r % 2
+    def arrived(r):
         @pl.when(y + z > 0)
         def _():
             each(NZ, lambda i: copy2(r, i, True).wait_recv())
@@ -236,35 +252,74 @@
         @pl.when(y + z == 0)
         def _():
             recv2[r] = jnp.zeros(recv2.shape[1:], BF16)
-        prefix = [recv2[r, o, 0:DH, :] for o in range(NZ)]
-        feats = [qf[h, half * 8 + o] for o in range(NZ)]
+
+    def read_out_first(half):
+        arrived(half)
+        prefix = [recv2[half, o, 0:DH, :] for o in range(NZ)]
+        feats = [qf[0, half * NZ + o] for o in range(NZ)]
         if half == 0:
             pieces = [recv2[0, o, DH:DH + EXTRA, :].astype(F32)[:8] for o in range(NZ)]
-            prefix.append(jnp.concatenate(pieces, axis=0).astype(BF16))
-            feats.append(qf[h, 16])
-        num[h] += nt(jnp.concatenate(prefix, axis=1), jnp.concatenate(feats, axis=1))
+            middles[...] = jnp.concatenate(pieces, axis=0).astype(BF16)
+            prefix.append(middles[...])
+            feats.append(qf[0, 16])
+        num[0] += nt(jnp.concatenate(prefix, axis=1), jnp.concatenate(feats, axis=1))
+
+    def read_out_second(r):
+        first, n = (0, FIRST) if r == 2 else (FIRST, DH - FIRST)
+        arrived(r)
+        prefix = [recv2[r, o, half * n:(half + 1) * n, :] for half in range(2) for o in range(NZ)]
+        prefix.append(middles[first:first + n, :])
+        feats = [qf[1, i] for i in range(17)]
+        num[1, first:first + n, :] += nt(jnp.concatenate(prefix, axis=1), jnp.concatenate(feats, axis=1))
 
     load(4).wait()
     gains = jnp.transpose(jnp.broadcast_to(gain_ref[...], (LANES, LANES)))
 
-    def normalise(h):
+    def gain_of(first, n):
+        return jnp.concatenate([gains[first:first + n]] * (tok // LANES), axis=1)
+
+    def inverse_norm(h):
         value = num[h]
-        meansq = jnp.mean(value * value, axis=0, keepdims=True)
-        gain = jnp.concatenate([gains[h * DH:(h + 1) * DH]] * (tok // LANES), axis=1)
-        ncat[h, me] = (value * lax.rsqrt(meansq + EPSILON) * gain).astype(BF16)
+        return lax.rsqrt(jnp.mean(value * value, axis=0, keepdims=True) + EPSILON)
+
+    def spread(h):
         each(NH // 2, lambda i: copy_n(h, i).start())
         copy_pair(h, 0).start()
+
+    def give_first():
+        ncat[me] = (num[0] * inverse_norm(0) * gain_of(0, DH)).astype(BF16)
+        spread(0)
+
+    def give_early():
+        early[me] = (num[1, 0:FIRST, :] * gain_of(DH, FIRST)).astype(BF16)
+        spread(1)
+
+    def give_last():
+        n = DH - FIRST
+        last[me, :, 0:tok] = (num[1, FIRST:DH, :] * gain_of(DH + FIRST, n)).astype(BF16)
+        flat = inverse_norm(1)
+        scale = jnp.concatenate([flat[:, i * LANES:(i + 1) * LANES] for i in range(tok // LANES)], axis=0)
+        high = scale.astype(BF16).astype(F32)
+        side = jnp.concatenate([high, scale - high, jnp.zeros((n - 8, LANES), F32)], axis=0)
+        last[me, :, tok:tok + LANES] = side.astype(BF16)
+        each(NH, lambda i: copy_last(i).start())
 
     def pass_on(h):
         for i in (1, 3, 2):
             copy_n(h, i, True).wait_recv()
             copy_pair(h, i).start()
 
-    def project(h):
+    def gathered(h):
         for i in range(NH // 2):
             copy_pair(h, i, True).wait_recv()
-        blocks = jnp.concatenate([ncat[h, s] for s in range(NH)], axis=0)
-        return nn(wt[:, h * NH * DH:(h + 1) * NH * DH], blocks)
+
+    def project_second(s):
+        block = jnp.concatenate([early[s], last[s, :, 0:tok]], axis=0)
+        side = last[s, :, tok:tok + LANES].astype(F32)
+        parts = tok // LANES
+        scale = side[0:parts] + side[parts:2 * parts]
+        flat = jnp.concatenate([scale[i:i + 1] for i in range(parts)], axis=1)
+        acc[...] += nn(wt2[s], block) * flat
 
     totals(0)
     totals(1)
@@ -275,20 +330,27 @@
     prefixes(2)
     each(NH, lambda i: copy_w(i, True).wait_recv())
     turned = [jnp.transpose(wbuf[s].astype(F32)) for s in range(NH)]
-    for h in range(2):
-        part = jnp.concatenate([t[:, h * DH:(h + 1) * DH] for t in turned], axis=1)
-        wt[:, h * NH * DH:(h + 1) * NH * DH] = part.astype(BF16)
+    wt[...] = jnp.concatenate([t[:, 0:DH] for t in turned], axis=1).astype(BF16)
+    for s in range(NH):
+        wt2[s] = turned[s][:, DH:].astype(BF16)
     prefixes(3)
-    read_out(0)
-    read_out(1)
-    normalise(0)
-    read_out(2)
+    read_out_first(0)
+    read_out_first(1)
+    give_first()
+    read_out_second(2)
+    give_early()
+    read_out_second(3)
+    give_last()
     pass_on(0)
-    read_out(3)
-    normalise(1)
-    acc[...] = project(0)
+    gathered(0)
+    acc[...] = nn(wt[...], jnp.concatenate([ncat[s] for s in range(NH)], axis=0))
     pass_on(1)
-    out_ref[...] = jnp.transpose(acc[...] + project(1)).astype(BF16)
+    gathered(1)
+    project_second(me)
+    for i in (1, 7, 2, 6, 3, 5, 4):
+        copy_last(i, True).wait_recv()
+        project_second(lax.rem(me + NH - i, NH))
+    out_ref[...] = jnp.transpose(acc[...]).astype(BF16)
 
     for r in range(ROUNDS):
         each(NZ, lambda i: copy1(r, i).wait_send())
@@ -307,11 +369,12 @@
         each(NH // 2, lambda i: copy_n(h, i).wait_send())
         for i in range(NH // 2):
             copy_pair(h, i).wait_send()
+    each(NH, lambda i: copy_last(i).wait_send())
 
 
 def per_device(queries, keys, values, gain, out_weight):
     tok, width = queries.shape
-    rows = DH + EXTRA
+    rows = max(ROWS)
     vmem = pl.BlockSpec(memory_space=pltpu.VMEM)
     dma = pltpu.SemaphoreType.DMA
     return pl.pallas_call(
@@ -333,9 +396,13 @@
             pltpu.VMEM((2, 17, tok, LANES), BF16),
             pltpu.VMEM((2, DH, tok), F32),
             pltpu.VMEM((NH, LANES, LANES), BF16),
-            pltpu.VMEM((LANES, NH * LANES), BF16),
+            pltpu.VMEM((LANES, NH * DH), BF16),
+            pltpu.VMEM((NH, LANES, DH), BF16),
             pltpu.VMEM((LANES, tok), F32),
-            pltpu.VMEM((2, NH, DH, tok), BF16),
+            pltpu.VMEM((DH, LANES), BF16),
+            pltpu.VMEM((NH, DH, tok), BF16),
+            pltpu.VMEM((NH, FIRST, tok), BF16),
+            pltpu.VMEM((NH, DH - FIRST, tok + LANES), BF16),
             pltpu.VMEM((ROUNDS, NZ, rows, LANES), BF16),
             pltpu.VMEM((ROUNDS, NZ, rows, LANES), BF16),
             pltpu.VMEM((ROUNDS, NY, rows, LANES), F32),
@@ -346,6 +413,7 @@
             dma((ROUNDS, NZ)), dma((ROUNDS, NZ)),
             dma((NH,)), dma((NH,)),
             dma((2, NH // 2)), dma((2, NH)), dma((2, NH // 2)),
+            dma((NH,)), dma((NH,)),
             dma((5,)),
         ],
         compiler_params=pltpu.CompilerParams(

time: 47.8 us -> 47.1 us (0.985)
  Pallas kernels: 46.4 us -> 45.7 us
    pallas_call x1, Pallas kernels: 46.4 us -> 45.7 us  [per_device(): pl.pallas_call(kernel, out_shape=jax.ShapeDtypeStruct((tok, width), BF16)...]
where the time goes in v2:
time: 47.1 us; the launch traced here: 47 us
  Pallas kernels  45.7 us (97%)
  local copies, waits for them, and re-layouts  1.31 us (3%)
    pallas_call x1, Pallas kernels, per_device(): pl.pallas_call(kernel, out_shape=jax.ShapeDtypeStruct((tok, width), BF16)...  45.7 us
    unnamed x3, local copies, waits for them, and re-layouts  1.31 us

profile of v2, /device:TPU:17, one launch (start us, length us, event | category | flops | bytes accessed | tf_op | source)
XLA Modules:
  0.0 47.0 jit_solution(16127986743833489191)
XLA Ops:
  0.0 0.0 copy-start
  0.0 0.7 %copy-done = f32[128]{0:T(128)S(1)} copy-done((f32[128]{0:T(128)S(1)}, f32[128]{0:T(128)}, u32[]{:S(2)}) %copy-start) | copy-done | bytes 536
  0.7 45.7 %shard_map.55 = bf16[512,128]{1,0:T(8,128)(2,1)S(1)} custom-call(bf16[512,128]{1,0:T(8,128)(2,1)} %q_hbm.1, bf16[512,128]{1,0:T(8,128)(2,1)} %k_hbm.1, bf16[512,128]{1,0:T(8,128)(2,1)} %v_hbm.1, f32[1,128]{1,0:T(1,128)S(1)} %bitcast.1, bf16[128,1024]{1,0:T(8,128)(2,1)} %w_hbm.1), custom_call_target="tpu_custom_call" | custom-call | tf_op jit(solution)/shard_map/pallas_call | solution.py:380
  46.3 0.7 %copy.7 = bf16[512,128]{1,0:T(8,128)(2,1)} copy(bf16[512,128]{1,0:T(8,128)(2,1)S(1)} %shard_map.55) | data formatting | bytes 262144
Async XLA Ops:
  0.0 0.7 %copy-start = (f32[128]{0:T(128)S(1)}, f32[128]{0:T(128)}, u32[]{:S(2)}) copy-start(f32[128]{0:T(128)} %param.8) | copy-start | bytes 1540

commit v3 on v2

--- a/solution.py
+++ b/solution.py
@@ -15,6 +15,7 @@
 NY = 4
 NH = 8
 ROUNDS = 4
+PAIRS = NZ // 2
 EXTRA = 16
 F32 = jnp.float32
 BF16 = jnp.bfloat16
@@ -37,11 +38,13 @@
 
 
 def kernel(q_hbm, k_hbm, v_hbm, gain_hbm, w_hbm, out_ref,
-           q_ref, k_ref, v_ref, gain_ref, w_ref, kx, kz, qx, qz, vt, qf, num, wbuf, wt, wt2, acc, middles, ncat, early, last, send1, recv1, ybuf, send2, recv2,
-           s1_send, s1_recv, y_send, y_recv, s2_send, s2_recv, w_send, w_recv, n_send, n_recv, p_send, l_send, l_recv, loaded):
+           q_ref, k_ref, v_ref, gain_ref, w_ref, kx, kz, qx, qz, vt, qf, num, wbuf, wt, wt2, acc, middles, ncat, early, last, send1, got1, sum1, recv1, ybuf, send2, got2, sum2, recv2,
+           a_send, a_recv, b_send, b_recv, y_send, y_recv, c_send, c_recv, d_send, d_recv, w_send, w_recv, n_send, n_recv, p_send, l_send, l_recv, loaded):
     ctx = lax.axis_index("ctx")
     y, z = ctx // NZ, lax.rem(ctx, NZ)
     me = lax.axis_index("head")
+    pair, even = z // 2, lax.rem(z, 2) == 0
+    side = 1 - 2 * lax.rem(z, 2)
     tok = q_ref.shape[0]
 
     def load(i):
@@ -97,17 +100,23 @@
     load(1).wait()
     vt[...] = jnp.transpose(v_ref[...].astype(F32)).astype(BF16)
 
+    def toward(k):
+        return lax.rem(z + side * k + 2 * NZ, NZ)
+
+    def place(o):
+        return lax.rem(side * (o - z) + 2 * NZ, NZ)
+
     def states(h, half):
         feats = jnp.concatenate(products(kx, kz, h, half * NZ, NZ), axis=1)
         state = nn(vt[h * DH:(h + 1) * DH, :], feats).astype(BF16)
         for o in range(NZ):
             piece = state[:, o * LANES:(o + 1) * LANES]
             if h == 0:
-                send1[half, o, 0:DH, :] = piece
+                send1[half, place(o), 0:DH, :] = piece
             else:
                 last = DH - FIRST
-                send1[2, o, half * FIRST:(half + 1) * FIRST, :] = piece[:FIRST]
-                send1[3, o, half * last:(half + 1) * last, :] = piece[FIRST:]
+                send1[2, place(o), half * FIRST:(half + 1) * FIRST, :] = piece[:FIRST]
+                send1[3, place(o), half * last:(half + 1) * last, :] = piece[FIRST:]
 
     def extra_state():
         feats = middle(k_ref[...].astype(F32), kx).astype(BF16)
@@ -115,7 +124,7 @@
         state = jnp.where(low[:DH], pair[:DH], pair[DH:])
         for o in range(NZ):
             piece = jnp.concatenate([state[8 * o:8 * o + 8], jnp.zeros((8, LANES), F32)], axis=0)
-            send1[0, o, DH:DH + EXTRA, :] = piece.astype(BF16)
+            send1[0, place(o), DH:DH + EXTRA, :] = piece.astype(BF16)
 
     def columns(i):
         return pl.ds(pl.multiple_of(i * LANES, LANES), LANES)
@@ -124,18 +133,49 @@
         return pltpu.make_async_remote_copy(
             src_ref=src, dst_ref=dst, send_sem=sends, recv_sem=recvs, device_id=peer, device_id_type=MESH)
 
-    def z_from(i, arriving):
-        return lax.rem(z + NZ - i, NZ) if arriving else z
-
-    def copy1(r, i, arriving=False):
-        o, s, n = lax.rem(z + i, NZ), z_from(i, arriving), rows_of(r)
-        return copy(send1.at[r, o, pl.ds(0, n)], recv1.at[r, s, pl.ds(0, n)],
-                    s1_send.at[r, o], s1_recv.at[r, s], z_peer(i))
-
-    def copy2(r, i, arriving=False):
-        o, s, n = lax.rem(z + i, NZ), z_from(i, arriving), rows_of(r)
-        return copy(send2.at[r, o, pl.ds(0, n)], recv2.at[r, s, pl.ds(0, n)],
-                    s2_send.at[r, o], s2_recv.at[r, s], z_peer(i))
+    def at_z(i):
+        return {"ctx": y * NZ + i}
+
+    def part(ref, r, i):
+        return ref.at[r, i, pl.ds(0, rows_of(r))]
+
+    def copy_a(r):
+        n = rows_of(r)
+        return copy(send1.at[r, pl.ds(1, 4), pl.ds(0, n)], got1.at[r, :, pl.ds(0, n)],
+                    a_send.at[r], a_recv.at[r], at_z(toward(1)))
+
+    def copy_b(r, j):
+        return copy(part(sum1, r, j - 1), part(recv1, r, pair),
+                    b_send.at[r, j - 1], b_recv.at[r, pair], at_z(toward(-j)))
+
+    def from_b(r, i):
+        p = lax.rem(pair + i, PAIRS)
+        return copy(part(sum1, r, i - 1), part(recv1, r, p),
+                    b_send.at[r, i - 1], b_recv.at[r, p], at_z(toward(-1)))
+
+    def gateway(j):
+        return toward(2) if j == 2 else toward(-j)
+
+    def copy_c(r, j):
+        to = gateway(j)
+        return copy(part(send2, r, to // 2), part(got2, r, j - 1),
+                    c_send.at[r, j - 1], c_recv.at[r, j - 1], at_z(to))
+
+    def copy_d(r, j):
+        owner = toward(-j)
+        return copy(part(sum2, r, j), part(recv2, r, owner),
+                    d_send.at[r, j], d_recv.at[r, owner], at_z(toward(1)))
+
+    def from_d(r, k):
+        owner = toward(k)
+        return copy(part(sum2, r, k - 1), part(recv2, r, owner),
+                    d_send.at[r, k - 1], d_recv.at[r, owner], at_z(toward(1)))
+
+    def needs_c(j):
+        return y + gateway(j) // 2 > 0
+
+    def needs_d():
+        return jnp.logical_or(y > 0, z != 1)
 
     def copy_y(r, i, arriving=False):
         o, n = lax.rem(y + i, NY), rows_of(r)
@@ -172,16 +212,17 @@
         lax.fori_loop(1, count, body, 0)
 
     extra_state()
-    for r in range(ROUNDS):
+    for r in range(3):
         if r < 2:
             states(0, r)
-        elif r == 2:
+        else:
             states(1, 0)
             states(1, 1)
         if r == 0:
             pl.semaphore_wait(barrier, NZ + NY + NH - 3)
-        each(NZ, lambda i: copy1(r, i).start())
-        recv1[r, z, 0:rows_of(r), :] = send1[r, z, 0:rows_of(r), :]
+        copy_a(r).start()
+        if r == 2:
+            copy_a(3).start()
     load(3).wait()
     each(NH, lambda i: copy_w(i).start())
     wbuf[me] = w_ref[:, columns(me)]
@@ -208,16 +249,26 @@
             weights = jnp.where(s_at <= t_at, scores * scores, 0.0).astype(BF16)
             num[h, :, first:first + 256] = nn(vt[h * DH:(h + 1) * DH, 0:seen], weights)
 
-    intra(0)
-    intra(1)
+
+    def combine(r):
+        n = rows_of(r)
+        copy_a(r).wait_recv()
+        for j in range(1, 4):
+            both = send1[r, NZ - j, 0:n, :].astype(F32) + got1[r, j, 0:n, :].astype(F32)
+            sum1[r, j - 1, 0:n, :] = both.astype(BF16)
+            copy_b(r, j).start()
 
     def totals(r):
         n = rows_of(r)
-        each(NZ, lambda i: copy1(r, i, True).wait_recv())
+        both = send1[r, 0, 0:n, :].astype(F32) + got1[r, 0, 0:n, :].astype(F32)
+        recv1[r, pair, 0:n, :] = both.astype(BF16)
+        for i in range(1, PAIRS):
+            from_b(r, i).wait_recv()
         total = recv1[r, 0, 0:n, :].astype(F32)
-        for s in range(1, NZ):
-            total += recv1[r, s, 0:n, :].astype(F32)
+        for p in range(1, PAIRS):
+            total += recv1[r, p, 0:n, :].astype(F32)
         ybuf[r, y, 0:n, :] = total
+
         def to_later(i):
             @pl.when(y + i < NY)
             def _():
@@ -226,6 +277,7 @@
 
     def prefixes(r):
         n = rows_of(r)
+
         def from_earlier(i):
             @pl.when(y >= i)
             def _():
@@ -234,20 +286,45 @@
         running = jnp.zeros((n, LANES), F32)
         for s in range(NY):
             running += jnp.where(s < y, ybuf[r, s, 0:n, :], 0.0)
-        for s in range(NZ):
-            send2[r, s, 0:n, :] = running.astype(BF16)
-            running += recv1[r, s, 0:n, :].astype(F32)
-        def give(i):
-            @pl.when(y + lax.rem(z + i, NZ) > 0)
-            def _():
-                copy2(r, i).start()
-        each(NZ, give)
-        recv2[r, z, 0:n, :] = send2[r, z, 0:n, :]
+        for p in range(PAIRS):
+            send2[r, p, 0:n, :] = running.astype(BF16)
+            running += recv1[r, p, 0:n, :].astype(F32)
+        for j in (3, 2, 1):
+            @pl.when(needs_c(j))
+            def _(j=j):
+                copy_c(r, j).start()
+        share(r, 0, z, send2[r, pair, 0:n, :], send1[r, 0, 0:n, :], got1[r, 0, 0:n, :])
+
+    def share(r, j, owner, before, mine, other):
+        n = rows_of(r)
+        after = (before.astype(F32) + jnp.where(even, mine, other).astype(F32)).astype(BF16)
+        recv2[r, owner, 0:n, :] = jnp.where(even, before, after)
+        sum2[r, j, 0:n, :] = jnp.where(even, after, before)
+
+        @pl.when(needs_d())
+        def _():
+            copy_d(r, j).start()
+
+    def relay(r):
+        n = rows_of(r)
+
+        @pl.when(y + pair > 0)
+        def _():
+            for j in range(1, 4):
+                copy_c(r, j).wait_recv()
+
+        @pl.when(y + pair == 0)
+        def _():
+            got2[r] = jnp.zeros(got2.shape[1:], BF16)
+
+        for j in range(1, 4):
+            share(r, j, toward(-j), got2[r, j - 1, 0:n, :], send1[r, NZ - j, 0:n, :], got1[r, j, 0:n, :])
 
     def arrived(r):
         @pl.when(y + z > 0)
         def _():
-            each(NZ, lambda i: copy2(r, i, True).wait_recv())
+            for k in range(1, 5):
+                from_d(r, k).wait_recv()
 
         @pl.when(y + z == 0)
         def _():
@@ -321,19 +398,26 @@
         flat = jnp.concatenate([scale[i:i + 1] for i in range(parts)], axis=1)
         acc[...] += nn(wt2[s], block) * flat
 
-    totals(0)
-    totals(1)
-    prefixes(0)
-    totals(2)
-    prefixes(1)
-    totals(3)
-    prefixes(2)
+    combine(0)
+    intra(0)
+    combine(1)
+    intra(1)
+    combine(2)
+    combine(3)
     each(NH, lambda i: copy_w(i, True).wait_recv())
     turned = [jnp.transpose(wbuf[s].astype(F32)) for s in range(NH)]
     wt[...] = jnp.concatenate([t[:, 0:DH] for t in turned], axis=1).astype(BF16)
     for s in range(NH):
         wt2[s] = turned[s][:, DH:].astype(BF16)
-    prefixes(3)
+    totals(0)
+    totals(1)
+    totals(2)
+    prefixes(0)
+    totals(3)
+    for r in range(1, ROUNDS):
+        prefixes(r)
+    for r in range(ROUNDS):
+        relay(r)
     read_out_first(0)
     read_out_first(1)
     give_first()
@@ -353,17 +437,24 @@
     out_ref[...] = jnp.transpose(acc[...]).astype(BF16)
 
     for r in range(ROUNDS):
-        each(NZ, lambda i: copy1(r, i).wait_send())
+        copy_a(r).wait_send()
+
         def sent(i, r=r):
             @pl.when(y + i < NY)
             def _():
                 copy_y(r, i).wait_send()
         each(NY, sent)
-        def given(i, r=r):
-            @pl.when(y + lax.rem(z + i, NZ) > 0)
-            def _():
-                copy2(r, i).wait_send()
-        each(NZ, given)
+        for j in range(1, 4):
+            copy_b(r, j).wait_send()
+
+            @pl.when(needs_c(j))
+            def _(r=r, j=j):
+                copy_c(r, j).wait_send()
+
+        @pl.when(needs_d())
+        def _(r=r):
+            for j in range(4):
+                copy_d(r, j).wait_send()
     each(NH, lambda i: copy_w(i).wait_send())
     for h in range(2):
         each(NH // 2, lambda i: copy_n(h, i).wait_send())
@@ -404,13 +495,19 @@
             pltpu.VMEM((NH, FIRST, tok), BF16),
             pltpu.VMEM((NH, DH - FIRST, tok + LANES), BF16),
             pltpu.VMEM((ROUNDS, NZ, rows, LANES), BF16),
+            pltpu.VMEM((ROUNDS, 4, rows, LANES), BF16),
+            pltpu.VMEM((ROUNDS, 3, rows, LANES), BF16),
+            pltpu.VMEM((ROUNDS, PAIRS, rows, LANES), BF16),
+            pltpu.VMEM((ROUNDS, NY, rows, LANES), F32),
+            pltpu.VMEM((ROUNDS, PAIRS, rows, LANES), BF16),
+            pltpu.VMEM((ROUNDS, 3, rows, LANES), BF16),
+            pltpu.VMEM((ROUNDS, 4, rows, LANES), BF16),
             pltpu.VMEM((ROUNDS, NZ, rows, LANES), BF16),
-            pltpu.VMEM((ROUNDS, NY, rows, LANES), F32),
-            pltpu.VMEM((ROUNDS, NZ, rows, LANES), BF16),
-            pltpu.VMEM((ROUNDS, NZ, rows, LANES), BF16),
-            dma((ROUNDS, NZ)), dma((ROUNDS, NZ)),
+            dma((ROUNDS,)), dma((ROUNDS,)),
+            dma((ROUNDS, 3)), dma((ROUNDS, PAIRS)),
             dma((ROUNDS, NY)), dma((ROUNDS, NY)),
-            dma((ROUNDS, NZ)), dma((ROUNDS, NZ)),
+            dma((ROUNDS, 3)), dma((ROUNDS, 3)),
+            dma((ROUNDS, 4)), dma((ROUNDS, NZ)),
             dma((NH,)), dma((NH,)),
             dma((2, NH // 2)), dma((2, NH)), dma((2, NH // 2)),
             dma((NH,)), dma((NH,)),

time: 47.1 us -> 45.4 us (0.964)
  Pallas kernels: 45.7 us -> 43.9 us
    pallas_call x1, Pallas kernels: 45.7 us -> 43.9 us  [per_device(): pl.pallas_call(kernel, out_shape=jax.ShapeDtypeStruct((tok, width), BF16)...]
where the time goes in v3:
time: 45.4 us; the launch traced here: 45.2 us
  Pallas kernels  43.9 us (97%)
  local copies, waits for them, and re-layouts  1.31 us (3%)
    pallas_call x1, Pallas kernels, per_device(): pl.pallas_call(kernel, out_shape=jax.ShapeDtypeStruct((tok, width), BF16)...  43.9 us
    unnamed x3, local copies, waits for them, and re-layouts  1.31 us

profile of v3, /device:TPU:17, one launch (start us, length us, event | category | flops | bytes accessed | tf_op | source)
XLA Modules:
  0.0 45.2 jit_solution(13359989885330490357)
XLA Ops:
  0.0 0.0 copy-start
  0.0 0.7 %copy-done = f32[128]{0:T(128)S(1)} copy-done((f32[128]{0:T(128)S(1)}, f32[128]{0:T(128)}, u32[]{:S(2)}) %copy-start) | copy-done | bytes 536
  0.7 43.9 %shard_map.55 = bf16[512,128]{1,0:T(8,128)(2,1)S(1)} custom-call(bf16[512,128]{1,0:T(8,128)(2,1)} %q_hbm.1, bf16[512,128]{1,0:T(8,128)(2,1)} %k_hbm.1, bf16[512,128]{1,0:T(8,128)(2,1)} %v_hbm.1, f32[1,128]{1,0:T(1,128)S(1)} %bitcast.1, bf16[128,1024]{1,0:T(8,128)(2,1)} %w_hbm.1), custom_call_target="tpu_custom_call" | custom-call | tf_op jit(solution)/shard_map/pallas_call | solution.py:471
  44.5 0.7 %copy.7 = bf16[512,128]{1,0:T(8,128)(2,1)} copy(bf16[512,128]{1,0:T(8,128)(2,1)S(1)} %shard_map.55) | data formatting | bytes 262144
Async XLA Ops:
  0.0 0.7 %copy-start = (f32[128]{0:T(128)S(1)}, f32[128]{0:T(128)}, u32[]{:S(2)}) copy-start(f32[128]{0:T(128)} %param.8) | copy-start | bytes 1540

commit v4 on v3

--- a/solution.py
+++ b/solution.py
@@ -253,7 +253,7 @@
     def combine(r):
         n = rows_of(r)
         copy_a(r).wait_recv()
-        for j in range(1, 4):
+        for j in (3, 2, 1):
             both = send1[r, NZ - j, 0:n, :].astype(F32) + got1[r, j, 0:n, :].astype(F32)
             sum1[r, j - 1, 0:n, :] = both.astype(BF16)
             copy_b(r, j).start()
@@ -267,7 +267,7 @@
         total = recv1[r, 0, 0:n, :].astype(F32)
         for p in range(1, PAIRS):
             total += recv1[r, p, 0:n, :].astype(F32)
-        ybuf[r, y, 0:n, :] = total
+        ybuf[r, y, 0:n, :] = total.astype(BF16)
 
         def to_later(i):
             @pl.when(y + i < NY)
@@ -285,7 +285,7 @@
         each(NY, from_earlier)
         running = jnp.zeros((n, LANES), F32)
         for s in range(NY):
-            running += jnp.where(s < y, ybuf[r, s, 0:n, :], 0.0)
+            running += jnp.where(s < y, ybuf[r, s, 0:n, :].astype(F32), 0.0)
         for p in range(PAIRS):
             send2[r, p, 0:n, :] = running.astype(BF16)
             running += recv1[r, p, 0:n, :].astype(F32)
@@ -308,16 +308,14 @@
     def relay(r):
         n = rows_of(r)
 
-        @pl.when(y + pair > 0)
-        def _():
-            for j in range(1, 4):
-                copy_c(r, j).wait_recv()
-
         @pl.when(y + pair == 0)
         def _():
             got2[r] = jnp.zeros(got2.shape[1:], BF16)
 
         for j in range(1, 4):
+            @pl.when(y + pair > 0)
+            def _(j=j):
+                copy_c(r, j).wait_recv()
             share(r, j, toward(-j), got2[r, j - 1, 0:n, :], send1[r, NZ - j, 0:n, :], got1[r, j, 0:n, :])
 
     def arrived(r):
@@ -360,7 +358,8 @@
         return lax.rsqrt(jnp.mean(value * value, axis=0, keepdims=True) + EPSILON)
 
     def spread(h):
-        each(NH // 2, lambda i: copy_n(h, i).start())
+        for i in (2, 1, 3):
+            copy_n(h, i).start()
         copy_pair(h, 0).start()
 
     def give_first():
@@ -379,7 +378,8 @@
         high = scale.astype(BF16).astype(F32)
         side = jnp.concatenate([high, scale - high, jnp.zeros((n - 8, LANES), F32)], axis=0)
         last[me, :, tok:tok + LANES] = side.astype(BF16)
-        each(NH, lambda i: copy_last(i).start())
+        for i in (4, 3, 5, 2, 6, 1, 7):
+            copy_last(i).start()
 
     def pass_on(h):
         for i in (1, 3, 2):
@@ -409,12 +409,9 @@
     wt[...] = jnp.concatenate([t[:, 0:DH] for t in turned], axis=1).astype(BF16)
     for s in range(NH):
         wt2[s] = turned[s][:, DH:].astype(BF16)
-    totals(0)
-    totals(1)
-    totals(2)
-    prefixes(0)
-    totals(3)
-    for r in range(1, ROUNDS):
+    for r in range(ROUNDS):
+        totals(r)
+    for r in range(ROUNDS):
         prefixes(r)
     for r in range(ROUNDS):
         relay(r)
@@ -498,7 +495,7 @@
             pltpu.VMEM((ROUNDS, 4, rows, LANES), BF16),
             pltpu.VMEM((ROUNDS, 3, rows, LANES), BF16),
             pltpu.VMEM((ROUNDS, PAIRS, rows, LANES), BF16),
-            pltpu.VMEM((ROUNDS, NY, rows, LANES), F32),
+            pltpu.VMEM((ROUNDS, NY, rows, LANES), BF16),
             pltpu.VMEM((ROUNDS, PAIRS, rows, LANES), BF16),
             pltpu.VMEM((ROUNDS, 3, rows, LANES), BF16),
             pltpu.VMEM((ROUNDS, 4, rows, LANES), BF16),

time: 45.4 us -> 43.8 us (0.965)
  Pallas kernels: 43.9 us -> 42 us
    pallas_call x1, Pallas kernels: 43.9 us -> 42 us  [per_device(): pl.pallas_call(kernel, out_shape=jax.ShapeDtypeStruct((tok, width), BF16)...]
where the time goes in v4:
time: 43.8 us; the launch traced here: 43.3 us
  Pallas kernels  42 us (96%)
  local copies, waits for them, and re-layouts  1.31 us (3%)
    pallas_call x1, Pallas kernels, per_device(): pl.pallas_call(kernel, out_shape=jax.ShapeDtypeStruct((tok, width), BF16)...  42 us
    unnamed x3, local copies, waits for them, and re-layouts  1.31 us

profile of v4, /device:TPU:17, one launch (start us, length us, event | category | flops | bytes accessed | tf_op | source)
XLA Modules:
  0.0 43.3 jit_solution(700745991346833343)
XLA Ops:
  0.0 0.0 copy-start
  0.0 0.7 %copy-done = f32[128]{0:T(128)S(1)} copy-done((f32[128]{0:T(128)S(1)}, f32[128]{0:T(128)}, u32[]{:S(2)}) %copy-start) | copy-done | bytes 536
  0.7 42.0 %shard_map.55 = bf16[512,128]{1,0:T(8,128)(2,1)S(1)} custom-call(bf16[512,128]{1,0:T(8,128)(2,1)} %q_hbm.1, bf16[512,128]{1,0:T(8,128)(2,1)} %k_hbm.1, bf16[512,128]{1,0:T(8,128)(2,1)} %v_hbm.1, f32[1,128]{1,0:T(1,128)S(1)} %bitcast.1, bf16[128,1024]{1,0:T(8,128)(2,1)} %w_hbm.1), custom_call_target="tpu_custom_call" | custom-call | tf_op jit(solution)/shard_map/pallas_call | solution.py:468
  42.6 0.7 %copy.7 = bf16[512,128]{1,0:T(8,128)(2,1)} copy(bf16[512,128]{1,0:T(8,128)(2,1)S(1)} %shard_map.55) | data formatting | bytes 262144
Async XLA Ops:
  0.0 0.7 %copy-start = (f32[128]{0:T(128)S(1)}, f32[128]{0:T(128)}, u32[]{:S(2)}) copy-start(f32[128]{0:T(128)} %param.8) | copy-start | bytes 1540

commit v5 on v4

--- a/solution.py
+++ b/solution.py
@@ -39,7 +39,7 @@
 
 def kernel(q_hbm, k_hbm, v_hbm, gain_hbm, w_hbm, out_ref,
            q_ref, k_ref, v_ref, gain_ref, w_ref, kx, kz, qx, qz, vt, qf, num, wbuf, wt, wt2, acc, middles, ncat, early, last, send1, got1, sum1, recv1, ybuf, send2, got2, sum2, recv2,
-           a_send, a_recv, b_send, b_recv, y_send, y_recv, c_send, c_recv, d_send, d_recv, w_send, w_recv, n_send, n_recv, p_send, l_send, l_recv, loaded):
+           a_send, a_recv, b_send, b_recv, y_send, y_recv, c_send, c_recv, d_send, d_recv, w_send, w_recv, n_send, n_recv, p_send, loaded):
     ctx = lax.axis_index("ctx")
     y, z = ctx // NZ, lax.rem(ctx, NZ)
     me = lax.axis_index("head")
@@ -191,19 +191,15 @@
         return copy(w_ref.at[:, columns(o)], wbuf.at[s], w_send.at[o], w_recv.at[s], h_peer(i))
 
     def copy_n(h, i, arriving=False):
-        s, held = head_from(2 * i, arriving), (ncat, early)[h]
+        s, held = head_from(2 * i, arriving), (ncat, early, last)[h]
         return copy(held.at[me], held.at[s], n_send.at[h, i], n_recv.at[h, s], h_peer(2 * i))
 
     sibling = {"head": me + 1 - 2 * lax.rem(me, 2)}
 
     def copy_pair(h, i, arriving=False):
-        mine, held = lax.rem(me + NH - 2 * i, NH), (ncat, early)[h]
+        mine, held = lax.rem(me + NH - 2 * i, NH), (ncat, early, last)[h]
         s = mine + 1 - 2 * lax.rem(me, 2) if arriving else mine
         return copy(held.at[mine], held.at[s], p_send.at[h, i], n_recv.at[h, s], sibling)
-
-    def copy_last(i, arriving=False):
-        s = head_from(i, arriving)
-        return copy(last.at[me], last.at[s], l_send.at[i], l_recv.at[s], h_peer(i))
 
     def each(count, do):
         def body(i, c):
@@ -339,13 +335,21 @@
             feats.append(qf[0, 16])
         num[0] += nt(jnp.concatenate(prefix, axis=1), jnp.concatenate(feats, axis=1))
 
-    def read_out_second(r):
+    def read_out_second(r, owners, whole):
         first, n = (0, FIRST) if r == 2 else (FIRST, DH - FIRST)
+        prefix = [recv2[r, o, half * n:(half + 1) * n, :] for half in range(2) for o in owners]
+        feats = [qf[1, half * NZ + o] for half in range(2) for o in owners]
+        if whole:
+            prefix.append(middles[first:first + n, :])
+            feats.append(qf[1, 16])
+        num[1, first:first + n, :] += nt(jnp.concatenate(prefix, axis=1), jnp.concatenate(feats, axis=1))
+
+    def read_out_near(r):
+        read_out_second(r, [z] + [toward(-j) for j in range(1, 4)], True)
+
+    def read_out_far(r):
         arrived(r)
-        prefix = [recv2[r, o, half * n:(half + 1) * n, :] for half in range(2) for o in range(NZ)]
-        prefix.append(middles[first:first + n, :])
-        feats = [qf[1, i] for i in range(17)]
-        num[1, first:first + n, :] += nt(jnp.concatenate(prefix, axis=1), jnp.concatenate(feats, axis=1))
+        read_out_second(r, [toward(k) for k in range(1, 5)], False)
 
     load(4).wait()
     gains = jnp.transpose(jnp.broadcast_to(gain_ref[...], (LANES, LANES)))
@@ -378,8 +382,7 @@
         high = scale.astype(BF16).astype(F32)
         side = jnp.concatenate([high, scale - high, jnp.zeros((n - 8, LANES), F32)], axis=0)
         last[me, :, tok:tok + LANES] = side.astype(BF16)
-        for i in (4, 3, 5, 2, 6, 1, 7):
-            copy_last(i).start()
+        spread(2)
 
     def pass_on(h):
         for i in (1, 3, 2):
@@ -418,19 +421,24 @@
     read_out_first(0)
     read_out_first(1)
     give_first()
-    read_out_second(2)
+    read_out_near(2)
+    read_out_near(3)
+    read_out_far(2)
     give_early()
-    read_out_second(3)
+    read_out_far(3)
     give_last()
     pass_on(0)
     gathered(0)
     acc[...] = nn(wt[...], jnp.concatenate([ncat[s] for s in range(NH)], axis=0))
     pass_on(1)
+    pass_on(2)
     gathered(1)
     project_second(me)
-    for i in (1, 7, 2, 6, 3, 5, 4):
-        copy_last(i, True).wait_recv()
-        project_second(lax.rem(me + NH - i, NH))
+    for i in range(1, NH // 2):
+        project_second(lax.rem(me + 2 * i, NH))
+    for i in range(NH // 2):
+        copy_pair(2, i, True).wait_recv()
+        project_second(lax.rem(me + NH - 2 * i, NH) + 1 - 2 * lax.rem(me, 2))
     out_ref[...] = jnp.transpose(acc[...]).astype(BF16)
 
     for r in range(ROUNDS):
@@ -453,11 +461,10 @@
             for j in range(4):
                 copy_d(r, j).wait_send()
     each(NH, lambda i: copy_w(i).wait_send())
-    for h in range(2):
+    for h in range(3):
         each(NH // 2, lambda i: copy_n(h, i).wait_send())
         for i in range(NH // 2):
             copy_pair(h, i).wait_send()
-    each(NH, lambda i: copy_last(i).wait_send())
 
 
 def per_device(queries, keys, values, gain, out_weight):
@@ -506,8 +513,7 @@
             dma((ROUNDS, 3)), dma((ROUNDS, 3)),
             dma((ROUNDS, 4)), dma((ROUNDS, NZ)),
             dma((NH,)), dma((NH,)),
-            dma((2, NH // 2)), dma((2, NH)), dma((2, NH // 2)),
-            dma((NH,)), dma((NH,)),
+            dma((3, NH // 2)), dma((3, NH)), dma((3, NH // 2)),
             dma((5,)),
         ],
         compiler_params=pltpu.CompilerParams(

time: 43.8 us -> 43.2 us (0.986)
  no operation moved by 1% of the time
where the time goes in v5:
time: 43.2 us; the launch traced here: 43.1 us
  Pallas kernels  41.8 us (97%)
  local copies, waits for them, and re-layouts  1.31 us (3%)
    pallas_call x1, Pallas kernels, per_device(): pl.pallas_call(kernel, out_shape=jax.ShapeDtypeStruct((tok, width), BF16)...  41.8 us
    unnamed x3, local copies, waits for them, and re-layouts  1.31 us

profile of v5, /device:TPU:17, one launch (start us, length us, event | category | flops | bytes accessed | tf_op | source)
XLA Modules:
  0.0 43.1 jit_solution(2708004551668593543)
XLA Ops:
  0.0 0.0 copy-start
  0.0 0.7 %copy-done = f32[128]{0:T(128)S(1)} copy-done((f32[128]{0:T(128)S(1)}, f32[128]{0:T(128)}, u32[]{:S(2)}) %copy-start) | copy-done | bytes 536
  0.7 41.8 %shard_map.55 = bf16[512,128]{1,0:T(8,128)(2,1)S(1)} custom-call(bf16[512,128]{1,0:T(8,128)(2,1)} %q_hbm.1, bf16[512,128]{1,0:T(8,128)(2,1)} %k_hbm.1, bf16[512,128]{1,0:T(8,128)(2,1)} %v_hbm.1, f32[1,128]{1,0:T(1,128)S(1)} %bitcast.1, bf16[128,1024]{1,0:T(8,128)(2,1)} %w_hbm.1), custom_call_target="tpu_custom_call" | custom-call | tf_op jit(solution)/shard_map/pallas_call | solution.py:475
  42.5 0.7 %copy.7 = bf16[512,128]{1,0:T(8,128)(2,1)} copy(bf16[512,128]{1,0:T(8,128)(2,1)S(1)} %shard_map.55) | data formatting | bytes 262144
Async XLA Ops:
  0.0 0.7 %copy-start = (f32[128]{0:T(128)S(1)}, f32[128]{0:T(128)}, u32[]{:S(2)}) copy-start(f32[128]{0:T(128)} %param.8) | copy-start | bytes 1540
